TPU v7x, 32 devices: a whole 2x2x4 slice. The times are simulated.
32 devices in a mesh: tm: 4 (over y, x), stream: 8 (over z, core).
Axes of the slice: x: 2, y: 2, z: 4, core: 2. Of those that a mesh axis runs over, the one named last changes fastest.
Arguments:
- tokens: bfloat16 [8, 512, 768], P('stream', 'tm'), may hold values from -6 to 6
- cotangent: bfloat16 [8, 512, 768], P('stream', 'tm'), may hold values from -6 to 6
- decay: float32 [8, 512, 24], P('stream', 'tm'), may hold values from 0.4 to 1, as said below
- in_w: bfloat16 [768, 3328], P('stream'), may hold values from -0.21875 to 0.21875
- out_w: bfloat16 [1536, 768], P('stream'), may hold values from -0.15625 to 0.15625
- conv_w: float32 [4, 1792], replicated, may hold values from -3 to 3
- dskip: float32 [24], replicated, may hold values from 0.5 to 2
- norm_w: float32 [1536], replicated, may hold values from 0.1 to 1.9
Outputs:
- out: bfloat16 [8, 512, 768], P('stream', 'tm')
- grad_tokens: bfloat16 [8, 512, 768], P('stream', 'tm')
- grad_out_t: float32 [768, 1536], P(('tm', 'stream'))
Inputs may be any that keep to these rules, and one draw needn't show every extreme that they name: decay lies strictly between 0 and 1.
All inputs are finite; a program needn't handle non-finite values.
Results may differ from a plain program's by a relative error of at most 0.015.
Values may be sent and summed in bfloat16 or wider, within the bound.
A program may use at most 128 MiB of HBM per device.

v0:
```python
import jax
import jax.numpy as jnp
from jax import lax
from jax.sharding import PartitionSpec as P

block_len = 128
working = lax.Precision.HIGH


def shifted(value, axis, steps):
    count = lax.axis_size(axis)
    initial, last = (max(0, -steps), min(count, count - steps))
    return lax.ppermute(value, axis, [(source, source + steps) for source in range(initial, last)])


def entering(value, axis, join, neutral):
    count, mine = (lax.axis_size(axis), lax.axis_index(axis))
    pieces = jax.tree.map(lambda part: lax.all_gather(part, axis), value)
    running = jax.tree.map(
        lambda part, zero: jnp.full_like(part, 0) + jnp.asarray(zero, part.dtype), value, neutral
    )

    def step(position, running):
        longer = join(running, jax.tree.map(lambda part: part[position], pieces))
        return jax.tree.map(lambda new, old: jnp.where(position < mine, new, old), longer, running)

    return lax.fori_loop(0, count - 1, step, running)


def carried_in(shard, axis, join, neutral):
    count = lax.axis_size(axis)
    place = lax.axis_index(axis)
    ahead = count - 1 - place
    gathered = jax.tree.map(
        lambda a, kind: lax.all_gather(a.astype(kind), axis),
        shard,
        jax.tree.map(lambda a: jnp.bfloat16 if a.dtype == jnp.float32 else a.dtype, shard),
    )
    state = jax.tree.map(lambda a, e: jnp.zeros_like(a) + jnp.asarray(e, a.dtype), shard, neutral)

    def one(step, state):
        source = count - 1 - step
        return join(
            state,
            jax.tree.map(
                lambda a, own: lax.dynamic_index_in_dim(a, source, 0, False).astype(own.dtype),
                gathered,
                shard,
            ),
        )

    return lax.fori_loop(0, ahead, one, state)


def conv_apply(extended, conv_weight):
    conv_taps = conv_weight.shape[0]
    row_count = extended.shape[0] - conv_taps + 1
    result = jnp.zeros((row_count, extended.shape[1]), jnp.float32)
    for offset in range(conv_taps):
        result = result + conv_weight[offset] * extended[offset : offset + row_count]
    return result


def block_ssm(carry_state, x_block, b_block, c_block, decay_log):
    cumulative = jnp.cumsum(decay_log, axis=0)
    carried = jnp.exp(cumulative)[:, :, None] * jnp.einsum(
        "tn,hpn->thp", c_block, carry_state, precision=working
    )
    scores = jnp.einsum("tn,sn->ts", c_block, b_block, precision=working)
    later_idx = lax.broadcasted_iota(jnp.int32, scores.shape, 0)
    earlier_idx = lax.broadcasted_iota(jnp.int32, scores.shape, 1)
    causal = (later_idx >= earlier_idx)[:, :, None]
    log_gap = cumulative[:, None, :] - cumulative[None, :, :]
    weight = jnp.where(causal, jnp.exp(jnp.where(causal, log_gap, 0.0)), 0.0) * scores[:, :, None]
    inside = jnp.einsum("tsh,shp->thp", weight, x_block, precision=working)
    fade_out = jnp.exp(cumulative[-1][None, :] - cumulative)
    added = jnp.einsum("shp,sn->hpn", fade_out[:, :, None] * x_block, b_block, precision=working)
    carry_state = jnp.exp(cumulative[-1])[:, None, None] * carry_state + added
    return (carried + inside, carry_state)


def local_scan(conv_out, decay_log, skip_gain, head_count, state_width):
    row_count = conv_out.shape[0]
    inner_width = conv_out.shape[1] - 2 * state_width
    head_dim = inner_width // head_count
    block_rows = min(block_len, row_count)
    blocks = row_count // block_rows
    x_all = conv_out[:, :inner_width].reshape(blocks, block_rows, head_count, head_dim)
    b_all = conv_out[:, inner_width : inner_width + state_width].reshape(
        blocks, block_rows, state_width
    )
    c_all = conv_out[:, inner_width + state_width :].reshape(blocks, block_rows, state_width)
    d_all = decay_log.reshape(blocks, block_rows, head_count)

    def advance(carry_state, pieces):
        outputs, carry_state = block_ssm(carry_state, pieces[0], pieces[1], pieces[2], pieces[3])
        return (carry_state, outputs)

    start_state = jnp.zeros((head_count, head_dim, state_width), jnp.float32)
    final_state, results = lax.scan(advance, start_state, (x_all, b_all, c_all, d_all))
    x_heads = conv_out[:, :inner_width].reshape(row_count, head_count, head_dim)
    outputs = results.reshape(row_count, head_count, head_dim) + skip_gain[None, :, None] * x_heads
    return (outputs.reshape(row_count, inner_width), final_state)


def gate_norm(ssm_out, gate_in, norm_gain):
    gated = ssm_out * jax.nn.silu(gate_in)
    factor = lax.rsqrt(jnp.mean(gated * gated, axis=-1, keepdims=True) + 1e-05)
    return gated * factor * norm_gain


def combine_carry(earlier, later):
    return (earlier[0] * later[0], later[0][:, None, None] * earlier[1] + later[1])


def shards(tokens, cotangent, decay, in_w, out_w, conv_w, dskip, norm_w):
    inputs = tokens[0]
    grad_out = cotangent[0]
    decay_log = jnp.log(decay[0])
    row_count = inputs.shape[0]
    head_count = dskip.shape[0]
    full_in, full_out = (
        lax.all_gather(in_w, "stream", axis=0, tiled=True),
        lax.all_gather(out_w, "stream", axis=0, tiled=True),
    )
    inner_width = full_out.shape[0]
    model_width = full_out.shape[1]
    proj_width = full_in.shape[1]
    state_width = (proj_width - 2 * inner_width) // 2
    head_dim = inner_width // head_count
    conv_taps = conv_w.shape[0]
    projected = jnp.dot(inputs, full_in, preferred_element_type=jnp.float32).astype(jnp.bfloat16)
    gate_in = projected[:, :inner_width].astype(jnp.float32)
    mix_in = projected[:, inner_width:]
    rim_rows = shifted(mix_in[row_count - conv_taps + 1 :], "tm", 1)
    extended = jnp.concatenate([rim_rows, mix_in], axis=0).astype(jnp.float32)

    def conv_part(values):
        return conv_apply(values, conv_w)

    pre_act, conv_back = jax.vjp(conv_part, extended)
    conv_low = jax.nn.silu(pre_act).astype(jnp.bfloat16)
    conv_out = lax.optimization_barrier(conv_low).astype(jnp.float32)

    def scan_part(values):
        return local_scan(values, decay_log, dskip, head_count, state_width)

    (ssm_local, state_local), ssm_back = jax.vjp(scan_part, conv_out)
    cumulative = jnp.cumsum(decay_log, axis=0)
    decay_total = jnp.exp(cumulative[-1])
    identity = (jnp.ones_like(decay_total), jnp.zeros_like(state_local))
    state_in = entering((decay_total, state_local), "tm", combine_carry, identity)[1]
    b_vecs = conv_out[:, inner_width : inner_width + state_width]
    c_vecs = conv_out[:, inner_width + state_width :]
    x_heads = conv_out[:, :inner_width].reshape(row_count, head_count, head_dim)
    growth = jnp.exp(cumulative)
    carried = growth[:, :, None] * jnp.einsum("tn,hpn->thp", c_vecs, state_in, precision=working)
    ssm_out = ssm_local + carried.reshape(row_count, inner_width)

    def norm_part(ssm_values, gate_values):
        return gate_norm(ssm_values, gate_values, norm_w)

    normed, norm_back = jax.vjp(norm_part, ssm_out, gate_in)
    normed_low = normed.astype(jnp.bfloat16)
    result = jnp.dot(normed_low, full_out, preferred_element_type=jnp.float32).astype(jnp.bfloat16)
    grad_normed = jnp.einsum("td,ed->te", grad_out, full_out, preferred_element_type=jnp.float32)
    grad_ssm, grad_gate = norm_back(grad_normed)
    grad_heads = grad_ssm.reshape(row_count, head_count, head_dim)
    weighted = growth[:, :, None] * grad_heads
    adjoint_local = jnp.einsum("thp,tn->hpn", weighted, c_vecs, precision=working)
    adjoint_in = carried_in((decay_total, adjoint_local), "tm", combine_carry, identity)[1]
    (grad_local,) = ssm_back((grad_ssm, jnp.zeros_like(state_local)))
    fade_out = jnp.exp(cumulative[-1][None, :] - cumulative)
    grad_x = fade_out[:, :, None] * jnp.einsum("hpn,tn->thp", adjoint_in, b_vecs, precision=working)
    grad_b = jnp.einsum(
        "thp,hpn->tn", fade_out[:, :, None] * x_heads, adjoint_in, precision=working
    )
    grad_c = jnp.einsum("thp,hpn->tn", weighted, state_in, precision=working)
    grad_conv = grad_local + jnp.concatenate(
        [grad_x.reshape(row_count, inner_width), grad_b, grad_c], axis=1
    )
    sigmoid_pre = jax.nn.sigmoid(pre_act)
    (grad_ext,) = conv_back(grad_conv * sigmoid_pre * (1.0 + pre_act * (1.0 - sigmoid_pre)))
    incoming = shifted(grad_ext[: conv_taps - 1], "tm", -1)
    grad_mix = grad_ext[conv_taps - 1 :] + jnp.pad(
        incoming, ((row_count - conv_taps + 1, 0), (0, 0))
    )
    grad_proj = jnp.concatenate([grad_gate, grad_mix], axis=1).astype(jnp.bfloat16)
    grad_tokens = jnp.einsum(
        "tj,dj->td", grad_proj, full_in, preferred_element_type=jnp.float32
    ).astype(jnp.bfloat16)
    n_time = lax.axis_size("tm")
    n_stream = lax.axis_size("stream")
    grad_scale = (n_time * n_stream * row_count) ** (-0.5)
    shard_rows = model_width // (n_stream * n_time)
    reordered = (
        grad_out.reshape(row_count, n_time, n_stream, shard_rows)
        .transpose(0, 2, 1, 3)
        .reshape(row_count, model_width)
    )
    partial_sum = lax.psum_scatter(
        jnp.einsum("td,te->de", reordered, normed_low, preferred_element_type=jnp.float32).astype(
            jnp.bfloat16
        ),
        "stream",
        scatter_dimension=0,
        tiled=True,
    )
    summed = lax.psum_scatter(partial_sum, "tm", scatter_dimension=0, tiled=True).astype(
        jnp.float32
    )
    return (result[None], grad_tokens[None], summed * grad_scale)


def solution(mesh):
    in_specs = (
        P("stream", "tm", None),
        P("stream", "tm", None),
        P("stream", "tm", None),
        P("stream", None),
        P("stream", None),
        P(),
        P(),
        P(),
    )
    out_specs = (P("stream", "tm", None), P("stream", "tm", None), P(("tm", "stream"), None))
    return jax.shard_map(shards, mesh=mesh, in_specs=in_specs, out_specs=out_specs, check_vma=False)
```

profile of v0, /device:TPU:0, one launch (start us, length us, event | category | flops | bytes accessed | tf_op | source)
XLA Modules:
  0.0 290.1 jit_solution(1542002735825916047)
XLA Ops:
  7.2 0.7 all-gather.9.cloned.1.call-update
  8.0 0.7 log_bitcast_fusion
  10.7 56.7 %all-gather.9.cloned.1.call-done = bf16[768,3328]{1,0:T(8,128)(2,1)} async-done(((bf16[96,3328]{1,0:T(8,128)(2,1)}), bf16[768,3328]{1,0:T(8,128)(2,1)}) %all-gather.9.cloned.1.call-update) | async-done | bytes 5111824 | tf_op jit(solution)/shard_map/all_gather | solution.py:123
  67.4 3.3 %convolution_convert_fusion = bf16[128,3328]{1,0:T(8,128)(2,1)S(1)} fusion(bf16[768,3328]{1,0:T(8,128)(2,1)} %all-gather.9.cloned.1.call-done, bf16[1,128,768]{2,1,0:T(8,128)(2,1)S(1)} %copy-done), kind=kOutput, calls=%fused_computation.5 | convolution fusion | flops 654737408 | bytes 6160384 | tf_op jit(solution)/shard_map/dot_general | solution.py:132
  70.7 3.4 %collective-permute-start = (bf16[3,1792]{1,0:T(4,128)(2,1)S(1)}, bf16[3,1792]{1,0:T(4,128)(2,1)S(1)}, u32[]{:S(2)}, u32[]{:S(2)}) collective-permute-start(bf16[3,1792]{1,0:T(4,128)(2,1)S(1)} %slice.89), channel_id=1, source_target_pairs={{0,8},{8,16},{16,24},{1,9},{9,17},{17,25},{2,10},{10,18},{18,26},{... | collective-permute-start | bytes 32264 | tf_op jit(solution)/shard_map/ppermute | solution.py:13
  74.3 1.2 collective-permute-done
  75.6 1.5 multiply_convert_fusion
  77.5 1.9 convolution_add_fusion
  79.5 0.7 all-gather.11.cloned.1.call-update
  80.9 0.9 copy.50
  81.8 0.7 mul.402
  82.6 9.6 %all-gather.2 = f32[4,1,24]{2,1,0:T(1,128)S(1)} all-gather(f32[1,1,24]{2,1,0:T(1,128)S(1)} %get-tuple-element.413), channel_id=1, replica_groups=mesh['tm'=4,'stream'=8] {'tm'}, dimensions={0}, use_global_device_ids=true | all-gather | bytes 480 | tf_op jit(solution)/shard_map/all_gather | solution.py:18
  92.2 0.9 copy.53
  93.3 2.4 fusion.8
  95.7 1.3 fusion.14
  97.0 2.4 copy.54
  99.3 23.9 %all-gather.13.cloned.1.call-done = f32[96,64,128]{2,1,0:T(8,128)} async-done(((f32[24,64,128]{2,1,0:T(8,128)}), f32[96,64,128]{2,1,0:T(8,128)}) %all-gather.13.cloned.1.call-update) | async-done | bytes 3145744 | tf_op jit(solution)/shard_map/all_gather | solution.py:18
  123.2 4.0 %while.21 = (s32[]{:T(128)}, f32[24,64,128]{2,1,0:T(8,128)S(1)}, s32[]{:T(128)}, f32[4,24]{1,0:T(4,128)S(1)}, f32[4,24,64,128]{3,2,1,0:T(8,128)}, /*index=5*/s32[]{:T(128)}, s32[]{:T(128)}) while((s32[]{:T(128)}, f32[24,64,128]{2,1,0:T(8,128)S(1)}, s32[]{:T(128)}, f32[4,24]{1,0:T(4,128)S(1)}, f32[4,24,64,128]{3,2,1,0:T(8,128)}, ...), condition=%wide.region_2.3_spmd.clone, body=%wide.region_1.2_spmd.clone.sunk | while | flops 786436 | bytes 2359697 | solution.py:27
  123.2 1.3 fusion.110
  124.5 1.3 fusion.110
  125.9 1.3 fusion.110
  127.2 1.3 convolution_multiply_fusion.3
  128.5 2.3 copy.57
  130.8 25.7 %all-gather.11.cloned.1.call-done = bf16[1536,768]{1,0:T(8,128)(2,1)} async-done(((bf16[192,768]{1,0:T(8,128)(2,1)}), bf16[1536,768]{1,0:T(8,128)(2,1)}) %all-gather.11.cloned.1.call-update) | async-done | bytes 2359312 | tf_op jit(solution)/shard_map/all_gather | solution.py:124
  156.5 3.2 %multiply_reduce_fusion = (f32[128]{0:T(128)S(1)}, f32[128]{0:T(128)S(1)}, f32[128,1536]{1,0:T(8,128)S(1)}, f32[128,1536]{1,0:T(8,128)S(1)}) fusion(bf16[128,3328]{1,0:T(8,128)(2,1)S(1)} %convolution_convert_fusion, f32[128,1536]{1,0:T(8,128)} %copy.57, f32[128,1536]{1,0:T(8,128)} %copy.54, bf16[128,1792]{1,0:T(8,128)(2,1)S(1)} %get-tuple-element.403, ...), kind=kOutput, calls=%fused_computation.65 | convolution fusion | flops 304938752 | bytes 6501376 | tf_op jit(solution)/shard_map/td,ed->te/dot_general | solution.py:166
  159.8 3.1 %broadcast_multiply_fusion.4 = (f32[128,1536]{1,0:T(8,128)}, f32[128,1536]{1,0:T(8,128)S(1)}, bf16[128,1536]{1,0:T(8,128)(2,1)}) fusion(f32[1536]{0:T(1024)S(1)} %mul.403, bf16[128,3328]{1,0:T(8,128)(2,1)} %copy-done.5, f32[128,1536]{1,0:T(8,128)S(1)} %get-tuple-element.402, f32[128]{0:T(128)S(1)} %get-tuple-element.416, ...), kind=kLoop, calls=%fused_computation.93 | loop fusion | flops 4521984 | bytes 5905408 | tf_op jit(solution)/shard_map/transpose(jvp())/mul | solution.py:102
  163.1 1.9 convolution_convert_fusion.2
  165.1 8.1 %all-gather.3 = bf16[4,1,24]{2,1,0:T(2,128)(2,1)S(1)} all-gather(bf16[1,1,24]{2,1,0:T(2,128)(2,1)S(1)} %copy-done.35), channel_id=1, replica_groups=mesh['tm'=4,'stream'=8] {'tm'}, dimensions={0}, use_global_device_ids=true | all-gather | bytes 240 | tf_op jit(solution)/shard_map/all_gather | solution.py:35
  173.2 1.7 copy.65
  175.5 0.9 mul.385
  176.4 2.3 copy.59
  178.7 0.9 copy.66
  179.6 1.2 dynamic-slice.2
  181.5 1.4 convolution_bitcast_fusion.2
  183.0 2.1 mul.434
  185.1 2.4 copy.60
  187.4 3.1 %fusion.1 = bf16[768,1536]{0,1:T(8,128)(2,1)} fusion(bf16[128,768]{0,1:T(8,128)(2,1)S(1)} %bitcast.130, f32[128,1536]{1,0:T(8,128)S(1)} %copy-done.2, f32[1536]{0:T(1024)} %param.19, f32[128]{0:T(128)S(1)} %get-tuple-element.417), kind=kOutput, calls=%fused_computation.7 | convolution fusion | flops 303759360 | bytes 3348992 | tf_op jit(solution)/shard_map/td,te->de/dot_general | solution.py:202
  190.5 4.3 %copy.72 = bf16[768,1536]{1,0:T(8,128)(2,1)} copy(bf16[768,1536]{0,1:T(8,128)(2,1)} %fusion.1) | data formatting | bytes 4718592
  194.8 0.8 convolution_bitcast_fusion
  195.8 2.2 fusion.2
  198.0 1.1 fusion.11
  199.1 1.1 fusion.15
  200.3 1.0 copy-done.8
  201.4 1.4 convolution_bitcast_fusion.3
  202.8 1.1 copy.61
  203.9 1.6 convolution_add_fusion.1
  205.6 1.5 convolution_add_fusion.2
  207.1 2.9 fusion.16
  210.1 3.8 %while.20 = (s32[]{:T(128)}, f32[24,64,128]{2,1,0:T(8,128)S(1)}, s32[]{:T(128)}, bf16[4,24]{1,0:T(4,128)(2,1)S(1)}, bf16[4,24,64,128]{3,2,1,0:T(8,128)(2,1)}, /*index=5*/s32[]{:T(128)}, s32[]{:T(128)}, s32[]{:T(128)}, s32[]{:T(128)}) while((s32[]{:T(128)}, f32[24,64,128]{2,1,0:T(8,128)S(1)}, s32[]{:T(128)}, bf16[4,24]{1,0:T(4,128)(2,1)S(1)}, ...), condition=%wide.region_7.8_spmd, body=%wide.region_6.7_spmd.sunk | while | flops 589854 | bytes 1966475 | solution.py:52
  210.1 1.2 convert_add_fusion.2
  211.4 1.2 convert_add_fusion.2
  212.6 1.2 convert_add_fusion.2
  213.9 1.1 convolution_multiply_fusion.1
  215.0 1.2 copy.62
  216.3 0.8 convolution_bitcast_fusion.1
  217.6 1.6 broadcast_multiply_fusion
  219.5 1.3 collective-permute-start.1
  221.1 4.2 %collective-permute-done.1 = f32[3,1792]{1,0:T(4,128)S(1)} collective-permute-done((f32[3,1792]{1,0:T(4,128)S(1)}, f32[3,1792]{1,0:T(4,128)S(1)}, u32[]{:S(2)}, u32[]{:S(2)}) %collective-permute-start.1) | collective-permute-done | bytes 21536 | tf_op jit(solution)/shard_map/ppermute | solution.py:13
  225.3 9.7 %reduce-scatter.5.cloned.1.call-done = bf16[96,1536]{1,0:T(8,128)(2,1)} async-done(((bf16[768,1536]{1,0:T(8,128)(2,1)}), bf16[96,1536]{1,0:T(8,128)(2,1)}) %reduce-scatter.5.cloned.1.call-update) | async-done | bytes 294928
  235.1 1.9 copy.73
  237.0 4.9 %fusion.17 = bf16[1,128,768]{2,1,0:T(8,128)(2,1)} fusion(bf16[768,3328]{1,0:T(8,128)(2,1)} %all-gather.9.cloned.1.call-done, bf16[128,1792]{1,0:T(8,128)(2,1)S(1)} %fusion.18, bf16[128,1536]{1,0:T(8,128)(2,1)S(1)} %copy-done.13), kind=kOutput, calls=%fused_computation.33 | convolution fusion | flops 656113664 | bytes 6160384 | tf_op jit(solution)/shard_map/tj,dj->td/dot_general | solution.py:189
  241.9 39.3 %all-reduce.12.cloned.1.call-done = bf16[96,1536]{0,1:T(8,128)(2,1)} async-done(((bf16[96,1536]{0,1:T(8,128)(2,1)}), bf16[96,1536]{0,1:T(8,128)(2,1)}) %all-reduce.12.cloned.1.call-update) | async-done | bytes 294928
  281.2 1.2 convert_multiply_fusion.2
  282.4 0.9 copy.67
  (115 shorter events, 6.3 us)
Async XLA Ops:
  7.2 60.2 %copy-start = (bf16[1,128,768]{2,1,0:T(8,128)(2,1)S(1)}, bf16[1,128,768]{2,1,0:T(8,128)(2,1)}, u32[]{:S(2)}) copy-start(bf16[1,128,768]{2,1,0:T(8,128)(2,1)} %param.12) | copy-start | bytes 589828
  7.2 60.2 %all-gather.9.cloned.1.call-start = ((), (), s32[]{:S(2)}) async-start(), calls=%async_computation.1 | async-start | bytes 5750784 | tf_op jit(solution)/shard_map/all_gather | solution.py:123
  7.9 115.3 %all-gather.13.cloned.1.call-start = ((), (), s32[]{:S(2)}) async-start(), calls=%async_computation.3 | async-start | bytes 3932160 | tf_op jit(solution)/shard_map/all_gather | solution.py:18
  10.7 63.4 %copy-start.31 = (f32[4,1792]{1,0:T(4,128)S(1)}, f32[4,1792]{1,0:T(4,128)}, u32[]{:S(2)}) copy-start(f32[4,1792]{1,0:T(4,128)} %param.17) | copy-start | bytes 86020
  70.7 85.8 %copy-start.5 = (bf16[128,3328]{1,0:T(8,128)(2,1)}, bf16[128,3328]{1,0:T(8,128)(2,1)S(1)}, u32[]{:S(2)}) copy-start(bf16[128,3328]{1,0:T(8,128)(2,1)S(1)} %convolution_convert_fusion) | copy-start | bytes 2555908
  70.7 4.8 %collective-permute-start = (bf16[3,1792]{1,0:T(4,128)(2,1)S(1)}, bf16[3,1792]{1,0:T(4,128)(2,1)S(1)}, u32[]{:S(2)}, u32[]{:S(2)}) collective-permute-start(bf16[3,1792]{1,0:T(4,128)(2,1)S(1)} %slice.89), channel_id=1, source_target_pairs={{0,8},{8,16},{16,24},{1,9},{9,17},{17,25},{2,10},{10,18},{18,26},{... | collective-permute-start | bytes 32264 | tf_op jit(solution)/shard_map/ppermute | solution.py:13
  74.2 2.9 %copy-start.19 = (f32[1792]{0:T(1024)}, f32[1792]{0:T(1024)S(1)}, u32[]{:S(2)}) copy-start(f32[1792]{0:T(1024)S(1)} %get-tuple-element.374) | copy-start | bytes 21508
  74.2 2.9 %copy-start.21 = (f32[1792]{0:T(1024)}, f32[1792]{0:T(1024)S(1)}, u32[]{:S(2)}) copy-start(f32[1792]{0:T(1024)S(1)} %get-tuple-element.375) | copy-start | bytes 21508
  74.2 2.9 %copy-start.23 = (f32[1792]{0:T(1024)}, f32[1792]{0:T(1024)S(1)}, u32[]{:S(2)}) copy-start(f32[1792]{0:T(1024)S(1)} %get-tuple-element.377) | copy-start | bytes 21508
  74.2 2.9 %copy-start.25 = (f32[1792]{0:T(1024)}, f32[1792]{0:T(1024)S(1)}, u32[]{:S(2)}) copy-start(f32[1792]{0:T(1024)S(1)} %get-tuple-element.376) | copy-start | bytes 21508
  77.1 79.4 %copy-start.3 = (bf16[128,1792]{1,0:T(8,128)(2,1)}, bf16[128,1792]{1,0:T(8,128)(2,1)S(1)}, u32[]{:S(2)}) copy-start(bf16[128,1792]{1,0:T(8,128)(2,1)S(1)} %get-tuple-element.403) | copy-start | bytes 1376260
  79.4 77.0 %all-gather.11.cloned.1.call-start = ((), (), s32[]{:S(2)}) async-start(), calls=%async_computation.2 | async-start | bytes 2654208 | tf_op jit(solution)/shard_map/all_gather | solution.py:124
  80.2 129.8 %all-gather.15.cloned.1.call-start = ((), (), s32[]{:S(2)}) async-start(), calls=%async_computation.4 | async-start | bytes 1966080 | tf_op jit(solution)/shard_map/all_gather | solution.py:35
  81.8 93.7 %copy-start.11 = (f32[128,24]{0,1:T(8,128)}, f32[128,24]{0,1:T(8,128)S(1)}, u32[]{:S(2)}) copy-start(f32[128,24]{0,1:T(8,128)S(1)} %copy.50) | copy-start | bytes 36868
  92.2 3.4 %copy-start.32 = (pred[128,128]{1,0:T(8,128)(4,1)}, pred[128,128]{1,0:T(8,128)(4,1)S(1)}, u32[]{:S(2)}) copy-start(pred[128,128]{1,0:T(8,128)(4,1)S(1)} %iota_compare_fusion) | copy-start | bytes 49156
  93.3 2.4 copy-start.27
  127.2 29.3 %copy-start.18 = (bf16[1,128,768]{2,1,0:T(8,128)(2,1)S(1)}, bf16[1,128,768]{2,1,0:T(8,128)(2,1)}, u32[]{:S(2)}) copy-start(bf16[1,128,768]{2,1,0:T(8,128)(2,1)} %param.13) | copy-start | bytes 589828
  127.2 29.3 %copy-start.29 = (f32[1536]{0:T(1024)S(1)}, f32[1536]{0:T(1024)}, u32[]{:S(2)}) copy-start(f32[1536]{0:T(1024)} %param.19) | copy-start | bytes 18436
  156.5 3.3 %copy-start.6 = (f32[128,1536]{1,0:T(8,128)S(1)}, f32[128,1536]{1,0:T(8,128)}, u32[]{:S(2)}) copy-start(f32[128,1536]{1,0:T(8,128)} %copy.54) | copy-start | bytes 2359300
  156.5 3.3 %copy-start.7 = (f32[128,1536]{1,0:T(8,128)S(1)}, f32[128,1536]{1,0:T(8,128)}, u32[]{:S(2)}) copy-start(f32[128,1536]{1,0:T(8,128)} %copy.57) | copy-start | bytes 2359300
  159.7 3.1 %copy-start.1 = (f32[128,1536]{1,0:T(8,128)}, f32[128,1536]{1,0:T(8,128)S(1)}, u32[]{:S(2)}) copy-start(f32[128,1536]{1,0:T(8,128)S(1)} %get-tuple-element.402) | copy-start | bytes 2359300
  162.9 2.2 copy-start.35
  165.1 70.0 %reduce-scatter.5.cloned.1.call-start = ((), (), s32[]{:S(2)}) async-start(), calls=%async_computation.5 | async-start | bytes 2654208
  185.1 2.4 copy-start.2
  190.5 4.3 %copy-start.12 = (f32[128,24]{0,1:T(8,128)S(1)}, f32[128,24]{0,1:T(8,128)}, u32[]{:S(2)}) copy-start(f32[128,24]{0,1:T(8,128)} %copy-done.11) | copy-start | bytes 36868
  194.8 1.0 copy-start.14
  195.8 2.2 copy-start.28
  195.8 2.2 copy-start.33
  195.8 2.2 copy-start.34
  200.2 1.1 copy-start.8
  200.3 3.7 %copy-start.16 = (f32[128,128]{1,0:T(8,128)S(1)}, f32[128,128]{1,0:T(8,128)}, u32[]{:S(2)}) copy-start(f32[128,128]{1,0:T(8,128)} %convolution_bitcast_fusion.2) | copy-start | bytes 196612
  200.3 80.9 %all-reduce.12.cloned.1.call-start = ((), (), s32[]{:S(2)}) async-start(), calls=%async_computation.6 | async-start | bytes 786432
  202.8 2.8 copy-start.17
  202.8 4.3 %copy-start.30 = (f32[1536]{0:T(1024)S(1)}, f32[1536]{0:T(1024)}, u32[]{:S(2)}) copy-start(f32[1536]{0:T(1024)} %param.19) | copy-start | bytes 18436
  207.1 3.0 %copy-start.36 = (bf16[4,1,24]{2,0,1:T(4,128)(2,1)S(1)}, bf16[4,1,24]{2,0,1:T(4,128)(2,1)}, u32[]{:S(2)}) copy-start(bf16[4,1,24]{2,0,1:T(4,128)(2,1)} %copy.78) | copy-start | bytes 580
  215.0 2.1 copy-start.4
  216.2 1.1 copy-start.9
  216.2 1.4 copy-start.10
  216.2 1.4 copy-start.15
  216.2 1.4 copy-start.26
  217.6 1.6 copy-start.20
  217.6 1.6 copy-start.22
  217.6 1.6 copy-start.24
  219.5 5.8 %collective-permute-start.1 = (f32[3,1792]{1,0:T(4,128)S(1)}, f32[3,1792]{1,0:T(4,128)S(1)}, u32[]{:S(2)}, u32[]{:S(2)}) collective-permute-start(f32[3,1792]{1,0:T(4,128)S(1)} %pad_add_fusion.1), channel_id=1, source_target_pairs={{8,0},{16,8},{24,16},{9,1},{17,9},{25,17},{10,2},{18,10},{26,18},{... | collective-permute-start | bytes 64520 | tf_op jit(solution)/shard_map/ppermute | solution.py:13
  221.1 15.9 %copy-start.13 = (bf16[128,1536]{1,0:T(8,128)(2,1)S(1)}, bf16[128,1536]{1,0:T(8,128)(2,1)}, u32[]{:S(2)}) copy-start(bf16[128,1536]{1,0:T(8,128)(2,1)} %get-tuple-element.405) | copy-start | bytes 1179652
Sparse Core Ops, SparseCore 0:
  9.7 57.6 all-gather.8
  79.5 43.5 all-gather.12
  124.8 31.6 all-gather.10
  165.2 30.0 all-gather.14
  200.4 34.6 reduce-scatter.4
  237.9 43.2 all-reduce.11
where the time goes:
time: 292 us; the launch traced here: 290 us
  waiting for transfers between devices  162 us (55%)
  matrix products  39.3 us (13%)
  local copies, waits for them, and re-layouts  31 us (11%)
  other arithmetic  19.7 us (7%)
  blocking collectives  17.7 us (6%)
  between operations  15.3 us (5%)
  starting transfers between devices  4.91 us (2%)
    all_gather x1, waiting for transfers between devices, shards(): lax.all_gather(in_w, 'stream', axis=0, tiled=True)  56.7 us
    unnamed x8, waiting for transfers between devices  50.5 us
    all_gather x1, waiting for transfers between devices, shards(): lax.all_gather(out_w, 'stream', axis=0, tiled=True)  25.7 us
    all_gather x1, waiting for transfers between devices, entering(): pieces = jax.tree.map(lambda part: lax.all_gather(part, axis), value)  23.9 us
    unnamed x80, local copies, waits for them, and re-layouts  12.5 us
    all_gather x1, blocking collectives, entering(): pieces = jax.tree.map(lambda part: lax.all_gather(part, axis), value)  9.6 us
    all_gather x1, blocking collectives, carried_in(): lax.all_gather(a.astype(kind), axis)  8.06 us
  transfers between devices with their start and end apart: 8, of which 7 were waited for; matrix products, arithmetic and copies ran while one was open for 24% of the time, Pallas kernels for 0%

commit v1 on v0

v1 whole, which is shorter than its diff:
```python
import functools

import jax
import jax.numpy as jnp
from jax import lax
from jax.experimental import pallas as pl
from jax.experimental.pallas import tpu as pltpu
from jax.sharding import PartitionSpec as P

MESH = pl.DeviceIdType.MESH
F32, BF16 = jnp.float32, jnp.bfloat16
EXACT = lax.Precision.HIGHEST


def mm(a, b):
    return lax.dot_general(a, b, (((1,), (0,)), ((), ())), preferred_element_type=F32)


def mm_nt(a, b):
    return lax.dot_general(a, b, (((1,), (1,)), ((), ())), preferred_element_type=F32)


def mm_tn(a, b):
    return lax.dot_general(a, b, (((0,), (0,)), ((), ())), preferred_element_type=F32)


def mm_exact(a, b):
    return lax.dot_general(
        a, b, (((1,), (0,)), ((), ())), preferred_element_type=F32, precision=EXACT
    )


def greet(peers):
    barrier = pltpu.get_barrier_semaphore()
    for axis, index in peers:
        pl.semaphore_signal(barrier, inc=1, device_id={axis: index}, device_id_type=MESH)
    pl.semaphore_wait(barrier, len(peers))


def others(axis, mine, count):
    return [(axis, lax.rem(mine + d, count)) for d in range(1, count)]


def gather_kernel(
    n_tm, n_stream, own_blocks,
    tok, cot, dec, win, wout,
    tok_all, cot_all, dec_all, win_all, wout_all,
    tm_send, tm_recv, in_send, in_recv, out_send, out_recv,
):
    t, s = lax.axis_index("tm"), lax.axis_index("stream")
    z, c = s // 2, s % 2
    pairs = n_stream // 2
    own_pairs = own_blocks // 2
    sibling = s + 1 - 2 * c
    greet(
        [
            ("stream", sibling),
            ("stream", lax.rem(z + 1, pairs) * 2 + c),
            ("stream", lax.rem(z + pairs - 1, pairs) * 2 + c),
        ]
        + others("tm", t, n_tm)
    )
    targets = (s + 2, s - 2, sibling)

    def in_copy(slot, way):
        return pltpu.make_async_remote_copy(
            src_ref=win_all.at[slot], dst_ref=win_all.at[slot],
            send_sem=in_send.at[way, slot], recv_sem=in_recv.at[slot],
            device_id={"stream": targets[way]}, device_id_type=MESH,
        )

    def out_copy(slot, way):
        at = slot - t * own_blocks
        return pltpu.make_async_remote_copy(
            src_ref=wout_all.at[at], dst_ref=wout_all.at[at],
            send_sem=out_send.at[way, at], recv_sem=out_recv.at[at],
            device_id={"stream": targets[way]}, device_id_type=MESH,
        )

    def held(pair):
        return (pair >= t * own_pairs) & (pair < (t + 1) * own_pairs)

    def tm_copy(kind, peer, slot):
        src, dst = ((tok, tok_all), (cot, cot_all), (dec, dec_all))[kind]
        return pltpu.make_async_remote_copy(
            src_ref=src, dst_ref=dst.at[slot],
            send_sem=tm_send.at[kind, peer], recv_sem=tm_recv.at[kind, slot],
            device_id={"tm": peer}, device_id_type=MESH,
        )

    def passes(copy, pair, fits, act):
        slot = 2 * pair + c

        @pl.when(fits & (pair <= z) & (z < pairs - 1))
        def _():
            act(copy(slot, 0))

        @pl.when(fits & (pair >= z) & (z > 0))
        def _():
            act(copy(slot, 1))

        @pl.when(fits)
        def _():
            act(copy(slot, 2))

    def start(copy):
        copy.start()

    win_all[s] = win[...]
    passes(in_copy, z, z >= 0, start)

    @pl.when(held(z))
    def _():
        wout_all[s - t * own_blocks] = wout[...]

    passes(out_copy, z, held(z), start)
    for kind in (0, 2, 1):
        for _, peer in others("tm", t, n_tm):
            tm_copy(kind, peer, t).start()
    tok_all[t] = tok[...]
    cot_all[t] = cot[...]
    dec_all[t] = dec[...]

    for j in range(1, pairs):
        for pair, inside in ((z - j, z - j >= 0), (z + j, z + j < pairs)):

            @pl.when(inside)
            def _(pair=pair):
                in_copy(2 * pair + c, 2).wait_recv()

            passes(in_copy, pair, inside, start)

            @pl.when(inside & held(pair))
            def _(pair=pair):
                out_copy(2 * pair + c, 2).wait_recv()

            passes(out_copy, pair, inside & held(pair), start)
    for pair in range(pairs):
        in_copy(2 * pair + 1 - c, 2).wait_recv()
    for j in range(own_pairs):
        out_copy(2 * (t * own_pairs + j) + 1 - c, 2).wait_recv()
    for kind in range(3):
        for _, peer in others("tm", t, n_tm):
            tm_copy(kind, peer, peer).wait_recv()
    for pair in range(pairs):
        passes(in_copy, pair, z >= 0, lambda copy: copy.wait_send())
    for pair in range(pairs):
        passes(out_copy, pair, held(pair), lambda copy: copy.wait_send())
    for kind in range(3):
        for _, peer in others("tm", t, n_tm):
            tm_copy(kind, peer, t).wait_send()


def sigmoid(v):
    return 1.0 / (1.0 + jnp.exp(-v))


def layer_kernel(
    n_tm, n_stream, inner, heads, head_dim, states, taps,
    tok, cot, dec, win, wout, par,
    out, grad_tok, grad_out_t,
    gate_s, ext_s, pre_s, x_s, b_s, c_s, g_s, f_s, el_s, ssm_s, gw_s, nb_s,
    mask_s, decay_s, start_s, fx_s, state_s,
    sums_s, osend, orecv, gsend, grecv, psend, precv, asend, arecv,
    s_send, s_recv, o_send, o_recv, g_send, g_recv, p_send, p_recv, a_send, a_recv,
):
    t, s = lax.axis_index("tm"), lax.axis_index("stream")
    blocks, rows, _ = tok.shape
    width = heads * head_dim
    model = tok.shape[2]
    all_heads = dec.shape[2]
    tm_peers = others("tm", t, n_tm)
    stream_peers = others("stream", s, n_stream)
    greet(tm_peers + stream_peers)

    def copy(src, dst, send, recv, axis, peer, at, slot):
        return pltpu.make_async_remote_copy(
            src_ref=src.at[at], dst_ref=dst.at[slot],
            send_sem=send.at[peer], recv_sem=recv.at[slot],
            device_id={axis: peer}, device_id_type=MESH,
        )

    def s_copy(peer, slot):
        return copy(sums_s, sums_s, s_send, s_recv, "tm", peer, t, slot)

    def o_copy(peer, slot):
        return copy(osend, orecv, o_send, o_recv, "tm", peer, peer, slot)

    def g_copy(peer, slot):
        return copy(gsend, grecv, g_send, g_recv, "tm", peer, peer, slot)

    def p_copy(peer, slot):
        return copy(psend, precv, p_send, p_recv, "stream", peer, peer, slot)

    def a_copy(peer, slot):
        return copy(asend, arecv, a_send, a_recv, "tm", peer, peer, slot)

    conv_w = [par[k : k + 1, :] for k in range(taps)]
    gain = par[taps : taps + 1, :width]
    skip = par[taps + 1 : taps + 2, :width]
    row_i = lax.broadcasted_iota(jnp.int32, (rows, rows), 0)
    col_i = lax.broadcasted_iota(jnp.int32, (rows, rows), 1)
    causal = row_i >= col_i
    tril = jnp.where(causal, 1.0, 0.0).astype(F32)
    pick_row = lax.broadcasted_iota(jnp.int32, (all_heads, width), 0) - t * heads
    pick_col = lax.broadcasted_iota(jnp.int32, (all_heads, width), 1)
    spread = jnp.where(
        (pick_col >= pick_row * head_dim) & (pick_col < (pick_row + 1) * head_dim), 1.0, 0.0
    ).astype(F32)
    one_row = lax.broadcasted_iota(jnp.int32, (all_heads, rows), 0) - t * heads
    one_col = lax.broadcasted_iota(jnp.int32, (all_heads, rows), 1)
    single = jnp.where(one_row == one_col, 1.0, 0.0).astype(F32)

    ext_s[0:8, :] = jnp.zeros((8, ext_s.shape[1]), F32)
    state_s[...] = jnp.zeros_like(state_s)

    def forward(q, carry):
        at = pl.multiple_of(q * rows, rows)
        here = pl.ds(at, rows)
        projected = mm(tok[q], win[...]).astype(BF16).astype(F32)
        gate = projected[:, :width]
        gate_s[here, :] = gate
        ext_s[pl.ds(pl.multiple_of(at + 8, 8), rows), :] = projected[:, width:]
        ext = ext_s[pl.ds(at, rows + 8), :]
        pre = conv_w[0] * ext[9 - taps : 9 - taps + rows]
        for k in range(1, taps):
            pre = pre + conv_w[k] * ext[9 - taps + k : 9 - taps + k + rows]
        pre_s[here, :] = pre
        conv = (pre * sigmoid(pre)).astype(BF16)
        x, b, c = conv[:, :width], conv[:, width : width + states], conv[:, width + states :]
        x_s[here, :] = x
        b_s[here, :] = b
        c_s[here, :] = c
        log_decay = jnp.log(dec[q])
        total = mm_exact(tril, mm_exact(log_decay, spread))
        across = mm_exact(tril, mm_exact(log_decay, single)).T
        last = total[rows - 1 : rows, :]
        grow = jnp.exp(total)
        fade = jnp.exp(last - total)
        g_s[here, :] = grow
        f_s[here, :] = fade
        end = jnp.exp(last)
        el_s[q] = jnp.broadcast_to(end, (8, width))
        x32 = x.astype(F32)
        faded = (fade * x32).astype(BF16)
        fx_s[here, :] = faded
        held = state_s[...]
        held_low = held.astype(BF16)
        start_s[q] = held_low
        state_s[...] = end * held + mm_tn(b, faded)
        scores = mm_nt(c, b)
        inside = []
        for h in range(heads):
            lo = h * head_dim
            gap = total[:, lo : lo + 1] - across[h : h + 1, :]
            weight = jnp.where(causal, jnp.exp(jnp.where(causal, gap, 0.0)), 0.0)
            decay_s[q * heads + h] = weight.astype(BF16)
            mix = (weight * scores).astype(BF16)
            mask_s[q * heads + h] = mix
            inside.append(mm(mix, x[:, lo : lo + head_dim]))
        ssm = jnp.concatenate(inside, axis=1) + grow * mm(c, held_low) + skip * x32
        ssm_s[here, :] = ssm
        gated = ssm * (gate * sigmoid(gate))
        weighted = mm_nt(cot[q], wout[...]) * gain
        gw_s[here, :] = weighted
        square = jnp.sum(gated * gated, axis=1, keepdims=True)
        cross = jnp.sum(weighted * gated, axis=1, keepdims=True)
        pair = jnp.where(col_i == 0, square, jnp.where(col_i == 1, cross, 0.0))
        sums_s[t, q] = pair.T[0:8, :]
        return carry

    lax.fori_loop(0, blocks, forward, 0)

    for _, peer in tm_peers:
        s_copy(peer, t).start()
    for _, peer in tm_peers:
        s_copy(peer, peer).wait_recv()

    def normed_rows(q):
        both = sums_s[0, q]
        for k in range(1, n_tm):
            both = both + sums_s[k, q]
        columns = jnp.concatenate([both, jnp.zeros((rows - 8, rows), F32)], axis=0).T
        factor = lax.rsqrt(columns[:, 0:1] * (1.0 / inner) + 1e-05)
        return factor, columns[:, 1:2]

    def outward(q, carry):
        here = pl.ds(pl.multiple_of(q * rows, rows), rows)
        factor, _ = normed_rows(q)
        gate = gate_s[here, :]
        normed = (ssm_s[here, :] * (gate * sigmoid(gate)) * factor * gain).astype(BF16)
        nb_s[here, :] = normed
        osend[q] = mm(normed, wout[...]).astype(BF16)

        @pl.when(q != t)
        def _():
            o_copy(q, t).start()

        return carry

    lax.fori_loop(0, blocks, outward, 0)

    share = model // n_stream
    part = share // n_tm
    product = mm_tn(cot[0], nb_s[0:rows, :])
    for q in range(1, blocks):
        product = product + mm_tn(cot[q], nb_s[q * rows : (q + 1) * rows, :])
    product = product.astype(BF16)
    to = lax.broadcasted_iota(jnp.int32, (model, model), 0)
    source = lax.broadcasted_iota(jnp.int32, (model, model), 1)
    owner = to // share
    within = to - owner * share
    slab = within // part
    wanted = slab * (part * n_stream) + owner * part + (within - slab * part)
    permute = jnp.where(source == wanted, 1.0, 0.0).astype(BF16)
    psend[...] = mm(permute, product).astype(BF16).reshape(n_stream, share, width)
    for _, peer in stream_peers:
        p_copy(peer, s).start()

    state_s[...] = jnp.zeros_like(state_s)

    def backward(step, carry):
        q = blocks - 1 - step
        at = pl.multiple_of(q * rows, rows)
        here = pl.ds(at, rows)
        factor, cross = normed_rows(q)
        gate = gate_s[here, :]
        ssm = ssm_s[here, :]
        sig = sigmoid(gate)
        silu = gate * sig
        gated = ssm * silu
        grad_gated = gw_s[here, :] * factor - gated * (
            factor * factor * factor * cross * (1.0 / inner)
        )
        grad_ssm = grad_gated * silu
        grad_gate = grad_gated * ssm * (sig * (1.0 + gate * (1.0 - sig)))
        x, b, c = x_s[here, :], b_s[here, :], c_s[here, :]
        low = grad_ssm.astype(BF16)
        grown = (g_s[here, :] * grad_ssm).astype(BF16)
        adjoint = state_s[...]
        adjoint_low = adjoint.astype(BF16)
        state_s[...] = el_s[q][0:1, :] * adjoint + mm_tn(c, grown)
        through = []
        gap = jnp.zeros((rows, rows), F32)
        for h in range(heads):
            lo = h * head_dim
            part_low = low[:, lo : lo + head_dim]
            through.append(mm_tn(mask_s[q * heads + h], part_low))
            gap = gap + mm_nt(part_low, x[:, lo : lo + head_dim]) * decay_s[
                q * heads + h
            ].astype(F32)
        gap = gap.astype(BF16)
        grad_x = (
            jnp.concatenate(through, axis=1)
            + f_s[here, :] * mm(b, adjoint_low)
            + skip * grad_ssm
        )
        grad_c = mm(gap, b) + mm_nt(grown, start_s[q])
        grad_b = mm_tn(gap, c) + mm_nt(fx_s[here, :], adjoint_low)
        pre = pre_s[here, :]
        sig_pre = sigmoid(pre)
        grad_pre = jnp.concatenate([grad_x, grad_b, grad_c], axis=1) * (
            sig_pre * (1.0 + pre * (1.0 - sig_pre))
        )
        ext = jnp.concatenate([grad_pre, carry], axis=0)
        grad_mix = conv_w[taps - 1] * ext[0:rows]
        for k in range(taps - 1):
            grad_mix = grad_mix + conv_w[k] * ext[taps - 1 - k : taps - 1 - k + rows]
        grad_proj = jnp.concatenate([grad_gate.astype(BF16), grad_mix.astype(BF16)], axis=1)
        gsend[q] = mm_nt(grad_proj, win[...]).astype(BF16)

        @pl.when(q != t)
        def _():
            g_copy(q, t).start()

        return grad_pre[0:8]

    lax.fori_loop(0, blocks, backward, jnp.zeros((8, width + 2 * states), F32))

    for _, peer in stream_peers:
        p_copy(peer, peer).wait_recv()
    total = psend[s].astype(F32)
    for _, peer in stream_peers:
        total = total + precv[peer].astype(F32)
    for k in range(n_tm):
        asend[k] = total[k * part : (k + 1) * part, :]
    for _, peer in tm_peers:
        a_copy(peer, t).start()
    for _, peer in tm_peers:
        o_copy(peer, peer).wait_recv()
    result = osend[t].astype(F32)
    for _, peer in tm_peers:
        result = result + orecv[peer].astype(F32)
    out[...] = result.astype(BF16)
    for _, peer in tm_peers:
        g_copy(peer, peer).wait_recv()
    result = gsend[t].astype(F32)
    for _, peer in tm_peers:
        result = result + grecv[peer].astype(F32)
    grad_tok[...] = result.astype(BF16)
    for _, peer in tm_peers:
        a_copy(peer, peer).wait_recv()
    arecv[t] = asend[t]
    scale = (n_stream * blocks * rows) ** (-0.5)
    grad_out_t[...] = (
        jnp.concatenate([arecv[k] for k in range(n_tm)], axis=1) * scale
    )
    for _, peer in tm_peers:
        s_copy(peer, t).wait_send()
        o_copy(peer, t).wait_send()
        g_copy(peer, t).wait_send()
        a_copy(peer, t).wait_send()
    for _, peer in stream_peers:
        p_copy(peer, s).wait_send()


def shards(n_tm, n_stream, tokens, cotangent, decay, in_w, out_w, conv_w, dskip, norm_w):
    t = lax.axis_index("tm")
    rows, model = tokens.shape[1:]
    all_heads = dskip.shape[0]
    inner = norm_w.shape[0]
    states = (in_w.shape[1] - 2 * inner) // 2
    taps = conv_w.shape[0]
    heads = all_heads // n_tm
    head_dim = inner // all_heads
    width = heads * head_dim
    wide = width + 2 * states
    span = width + wide

    def mine(a, axis, offset=0):
        return lax.dynamic_slice_in_dim(a, offset + t * width, width, axis)

    win = jnp.concatenate(
        [mine(in_w, 1), mine(in_w, 1, inner), in_w[:, 2 * inner :]], axis=1
    )
    tail = jnp.zeros((2 * states,), F32)
    skip = jnp.repeat(lax.dynamic_slice_in_dim(dskip, t * heads, heads), head_dim)
    par = jnp.concatenate(
        [
            jnp.concatenate([mine(conv_w, 1), conv_w[:, inner:]], axis=1),
            jnp.concatenate([mine(norm_w, 0), tail])[None],
            jnp.concatenate([skip, tail])[None],
        ]
    )
    own_blocks = width // out_w.shape[0]
    vmem = pl.BlockSpec(memory_space=pltpu.VMEM)
    dma = pltpu.SemaphoreType.DMA
    gathered = pl.pallas_call(
        functools.partial(gather_kernel, n_tm, n_stream, own_blocks),
        out_shape=[
            jax.ShapeDtypeStruct((n_tm, rows, model), BF16),
            jax.ShapeDtypeStruct((n_tm, rows, model), BF16),
            jax.ShapeDtypeStruct((n_tm, rows, all_heads), F32),
            jax.ShapeDtypeStruct((n_stream, in_w.shape[0], span), BF16),
            jax.ShapeDtypeStruct((own_blocks, out_w.shape[0], model), BF16),
        ],
        in_specs=[vmem] * 5,
        out_specs=[vmem] * 5,
        scratch_shapes=[
            dma((3, n_tm)), dma((3, n_tm)), dma((3, n_stream)), dma((n_stream,)),
            dma((3, own_blocks)), dma((own_blocks,)),
        ],
        compiler_params=pltpu.CompilerParams(
            collective_id=0, has_side_effects=True, vmem_limit_bytes=32 * 2**20
        ),
        name="gather",
    )(tokens[0], cotangent[0], decay[0], win, out_w)
    tok, cot, dec, win, wout = gathered
    win = win.reshape(model, span)
    wout = wout.reshape(width, model)
    length = n_tm * rows
    share = model // n_stream
    part = share // n_tm
    V = pltpu.VMEM
    out, grad_tok, grad_out_t = pl.pallas_call(
        functools.partial(
            layer_kernel, n_tm, n_stream, inner, heads, head_dim, states, taps
        ),
        out_shape=[
            jax.ShapeDtypeStruct((rows, model), BF16),
            jax.ShapeDtypeStruct((rows, model), BF16),
            jax.ShapeDtypeStruct((part, inner), F32),
        ],
        in_specs=[vmem] * 6,
        out_specs=[vmem] * 3,
        scratch_shapes=[
            V((length, width), F32), V((length + 8, wide), F32), V((length, wide), F32),
            V((length, width), BF16), V((length, states), BF16),
            V((length, states), BF16), V((length, width), F32), V((length, width), F32),
            V((n_tm, 8, width), F32), V((length, width), F32), V((length, width), F32),
            V((length, width), BF16), V((n_tm * heads, rows, rows), BF16),
            V((n_tm * heads, rows, rows), BF16), V((n_tm, states, width), BF16),
            V((length, width), BF16), V((states, width), F32),
            V((n_tm, n_tm, 8, rows), F32),
            V((n_tm, rows, model), BF16), V((n_tm, rows, model), BF16),
            V((n_tm, rows, model), BF16), V((n_tm, rows, model), BF16),
            V((n_stream, share, width), BF16), V((n_stream, share, width), BF16),
            V((n_tm, part, width), F32), V((n_tm, part, width), F32),
            dma((n_tm,)), dma((n_tm,)), dma((n_tm,)), dma((n_tm,)), dma((n_tm,)), dma((n_tm,)),
            dma((n_stream,)), dma((n_stream,)), dma((n_tm,)), dma((n_tm,)),
        ],
        compiler_params=pltpu.CompilerParams(
            collective_id=1, has_side_effects=True, vmem_limit_bytes=48 * 2**20
        ),
        name="layer",
    )(tok, cot, dec, win, wout, par)
    return out[None], grad_tok[None], grad_out_t


def solution(mesh):
    in_specs = (
        P("stream", "tm", None),
        P("stream", "tm", None),
        P("stream", "tm", None),
        P("stream", None),
        P("stream", None),
        P(),
        P(),
        P(),
    )
    out_specs = (P("stream", "tm", None), P("stream", "tm", None), P(("tm", "stream"), None))
    return jax.shard_map(
        functools.partial(shards, mesh.shape["tm"], mesh.shape["stream"]),
        mesh=mesh, in_specs=in_specs, out_specs=out_specs, check_vma=False,
    )
```

time: 292 us -> 77.8 us (0.27)
  waiting for transfers between devices: 162 us -> 0 us
  Pallas kernels: 0 us -> 66.2 us
  matrix products: 39.3 us -> 0 us
  local copies, waits for them, and re-layouts: 31 us -> 10.4 us
  other arithmetic: 19.7 us -> 0.03 us
  blocking collectives: 17.7 us -> 0 us
  between operations: 15.3 us -> 0.68 us
  starting transfers between devices: 4.91 us -> 0 us
    all_gather x4 -> x0, waiting for transfers between devices: 106 us -> none  [the longest x1 56.7 us: shards(): lax.all_gather(in_w, 'stream', axis=0, tiled=True)]
    pallas_call x0 -> x2, Pallas kernels: none -> 66.2 us  [the longest x1 38.2 us: shards(): pl.pallas_call(functools.partial(layer_kernel, n_tm, n_stream, inner, hea...]
    unnamed x8 -> x0, waiting for transfers between devices: 50.5 us -> none
    dot_general x21 -> x0, matrix products: 39.3 us -> none  [the longest x3 5.59 us: block_ssm(): inside = jnp.einsum('tsh,shp->thp', weight, x_block, precision=working)]
    all_gather x2 -> x0, blocking collectives: 17.7 us -> none  [the longest x1 9.6 us: entering(): pieces = jax.tree.map(lambda part: lax.all_gather(part, axis), value)]
    mul x6 -> x0, other arithmetic: 8.67 us -> none  [the longest x1 3.09 us: local_scan(): skip_gain[None, :, None] * x_heads]
    reshape x4 -> x1, local copies, waits for them, and re-layouts: 7.03 us -> 0.08 us  [shards(): jnp.repeat(lax.dynamic_slice_in_dim(dskip, t * heads, heads), head_dim)]
    unnamed x80 -> x10, local copies, waits for them, and re-layouts: 12.5 us -> 5.63 us
  transfers between devices with their start and end apart: 8 -> 0, of which waited for: 7 -> 0; matrix products, arithmetic and copies ran while one was open for 24% -> 0% of each run, Pallas kernels for 0% -> 0%
where the time goes in v1:
time: 77.8 us; the launch traced here: 77.3 us
  Pallas kernels  66.2 us (85%)
  local copies, waits for them, and re-layouts  10.4 us (13%)
    pallas_call x1, Pallas kernels, shards(): pl.pallas_call(functools.partial(layer_kernel, n_tm, n_stream, inner, hea...  38.2 us
    pallas_call x1, Pallas kernels, shards(): pl.pallas_call(functools.partial(gather_kernel, n_tm, n_stream, own_block...  27.9 us
    unnamed x10, local copies, waits for them, and re-layouts  5.63 us
    dynamic_slice x3, local copies, waits for them, and re-layouts, mine(): return lax.dynamic_slice_in_dim(a, offset + t * width, width, axis)  2.41 us

profile of v1, /device:TPU:0, one launch (start us, length us, event | category | flops | bytes accessed | tf_op | source)
XLA Modules:
  0.0 77.3 jit_solution(5561524291528783232)
XLA Ops:
  0.6 0.7 dynamic_slice.19
  1.4 0.8 dynamic_slice.18
  2.2 0.1 broadcast_in_dim.17
  2.2 0.1 reshape.17
  2.3 0.7 slice.7
  3.0 0.7 constant_dynamic-slice_fusion
  3.7 0.8 %slice.6 = bf16[96,256]{1,0:T(8,128)(2,1)S(1)} slice(bf16[96,3328]{1,0:T(8,128)(2,1)} %param.11), slice={[0:96], [3072:3328]} | slice | bytes 98304 | tf_op jit(solution)/shard_map/slice | solution.py:434
  4.5 0.8 %copy.11 = f32[1,128,24]{2,1,0:T(8,128)S(1)} copy(f32[1,128,24]{1,2,0:T(8,128)} %param.10) | data formatting | bytes 24576 | tf_op args[2]
  5.3 0.9 %constant_dynamic-slice_fusion.2 = (bf16[96,384]{1,0:T(8,128)(2,1)S(1)}, bf16[96,384]{1,0:T(8,128)(2,1)S(1)}) fusion(bf16[96,3328]{1,0:T(8,128)(2,1)} %param.11, s32[]{:T(128)S(6)} %select_n.15, s32[]{:T(128)S(6)} %select_n.16), kind=kLoop, calls=%fused_computation.4 | loop fusion | bytes 294920 | tf_op jit(solution)/shard_map/dynamic_slice | solution.py:431
  6.3 0.0 copy-start
  6.3 1.0 %copy-done = bf16[192,768]{1,0:T(8,128)(2,1)S(1)} copy-done((bf16[192,768]{1,0:T(8,128)(2,1)S(1)}, bf16[192,768]{1,0:T(8,128)(2,1)}, u32[]{:S(2)}) %copy-start) | copy-done | bytes 294936
  7.3 0.0 copy-start.1
  7.3 0.9 %copy-done.1 = bf16[1,128,768]{2,1,0:T(8,128)(2,1)S(1)} copy-done((bf16[1,128,768]{2,1,0:T(8,128)(2,1)S(1)}, bf16[1,128,768]{2,1,0:T(8,128)(2,1)}, u32[]{:S(2)}) %copy-start.1) | copy-done | bytes 196632
  8.2 0.0 copy-start.2
  8.2 0.9 %copy-done.2 = bf16[1,128,768]{2,1,0:T(8,128)(2,1)S(1)} copy-done((bf16[1,128,768]{2,1,0:T(8,128)(2,1)S(1)}, bf16[1,128,768]{2,1,0:T(8,128)(2,1)}, u32[]{:S(2)}) %copy-start.2) | copy-done | bytes 196632
  9.1 27.9 %gather.1 = (bf16[4,128,768]{2,1,0:T(8,128)(2,1)S(1)}, bf16[4,128,768]{2,1,0:T(8,128)(2,1)S(1)}, f32[4,128,24]{2,1,0:T(8,128)S(1)}, bf16[8,96,1024]{2,1,0:T(8,128)(2,1)S(1)}, bf16[2,192,768]{2,1,0:T(8,128)(2,1)S(1)}) custom-call(bf16[128,768]{1,0:T(8,128)(2,1)S(1)} %bitcast.12, bf16[128,768]{1,0:T(8,128)(2,1)S(1)} %bitcast.13, f32[128,24]{1,0:T(8,128)S(1)} %bitcast.9, ...), custom_call_target="tpu_custom_call" | custom-call | tf_op jit(solution)/shard_map/gather/pallas_call | solution.py:448
  37.0 38.2 %layer.1 = (bf16[128,768]{1,0:T(8,128)(2,1)S(1)}, bf16[128,768]{1,0:T(8,128)(2,1)S(1)}, f32[24,1536]{1,0:T(8,128)S(1)}) custom-call(bf16[4,128,768]{2,1,0:T(8,128)(2,1)S(1)} %get-tuple-element.11.tok, bf16[4,128,768]{2,1,0:T(8,128)(2,1)S(1)} %get-tuple-element.12.cot, f32[4,128,24]{2,1,0:T(8,128)S(1)} %get-tuple-element.13.dec, ...), custom_call_target="tpu_custom_call" | custom-call | tf_op jit(solution)/shard_map/layer/pallas_call | solution.py:475
  75.3 0.7 copy.15
  76.0 0.7 copy.16
  76.7 0.7 copy.17
  (6 shorter events, 0.1 us)
Async XLA Ops:
  6.3 1.0 %copy-start = (bf16[192,768]{1,0:T(8,128)(2,1)S(1)}, bf16[192,768]{1,0:T(8,128)(2,1)}, u32[]{:S(2)}) copy-start(bf16[192,768]{1,0:T(8,128)(2,1)} %wout.1) | copy-start | bytes 884740
  7.3 0.9 %copy-start.1 = (bf16[1,128,768]{2,1,0:T(8,128)(2,1)S(1)}, bf16[1,128,768]{2,1,0:T(8,128)(2,1)}, u32[]{:S(2)}) copy-start(bf16[1,128,768]{2,1,0:T(8,128)(2,1)} %param.8) | copy-start | bytes 589828
  8.2 0.9 %copy-start.2 = (bf16[1,128,768]{2,1,0:T(8,128)(2,1)S(1)}, bf16[1,128,768]{2,1,0:T(8,128)(2,1)}, u32[]{:S(2)}) copy-start(bf16[1,128,768]{2,1,0:T(8,128)(2,1)} %param.9) | copy-start | bytes 589828

commit v2 on v1

v2 whole, which is shorter than its diff:
```python
import functools

import jax
import jax.numpy as jnp
from jax import lax
from jax.experimental import pallas as pl
from jax.experimental.pallas import tpu as pltpu
from jax.sharding import PartitionSpec as P

MESH = pl.DeviceIdType.MESH
F32, BF16 = jnp.float32, jnp.bfloat16
EXACT = lax.Precision.HIGHEST


def mm(a, b):
    return lax.dot_general(a, b, (((1,), (0,)), ((), ())), preferred_element_type=F32)


def mm_nt(a, b):
    return lax.dot_general(a, b, (((1,), (1,)), ((), ())), preferred_element_type=F32)


def mm_tn(a, b):
    return lax.dot_general(a, b, (((0,), (0,)), ((), ())), preferred_element_type=F32)


def mm_exact(a, b, over=1):
    return lax.dot_general(
        a, b, (((over,), (0,)), ((), ())), preferred_element_type=F32, precision=EXACT
    )


def greet(peers):
    barrier = pltpu.get_barrier_semaphore()
    for axis, index in peers:
        pl.semaphore_signal(barrier, inc=1, device_id={axis: index}, device_id_type=MESH)
    pl.semaphore_wait(barrier, len(peers))


def others(axis, mine, count):
    return [(axis, lax.rem(mine + d, count)) for d in range(1, count)]


def sigmoid(v):
    return 1.0 / (1.0 + jnp.exp(-v))


def layer_kernel(
    n_tm, n_stream, inner, heads, head_dim, states, taps,
    tok_in, cot_in, dec_in, win_in, wout_in, conv_in, gain_in, skip_in,
    out, grad_tok, grad_out_t,
    tok, cot, dec, win_own, win_all, wout_all, win, wout, par, permute,
    gate_s, pre_s, x_s, b_s, c_s, g_s, f_s, el_s, ssm_s, gw_s, nb_s,
    mask_s, decay_s, start_s, fx_s, state_s,
    sums_s, osend, orecv, gsend, grecv, psend, precv, asend, arecv,
    local, tm_send, tm_recv, in_send, in_recv, out_send, out_recv,
    s_send, s_recv, o_send, o_recv, g_send, g_recv, p_send, p_recv, a_send, a_recv,
):
    t, s = lax.axis_index("tm"), lax.axis_index("stream")
    z, c = s // 2, s % 2
    pairs = n_stream // 2
    blocks, rows, model = tok.shape
    width = heads * head_dim
    all_heads = dec.shape[1]
    own_blocks = wout_all.shape[0]
    own_pairs = own_blocks // 2
    sibling = s + 1 - 2 * c
    tm_peers = others("tm", t, n_tm)
    stream_peers = others("stream", s, n_stream)

    def held(pair):
        return (pair >= t * own_pairs) & (pair < (t + 1) * own_pairs)

    own_win = pltpu.make_async_copy(win_in, win_own, local.at[0])
    own_win.start()
    stays = [
        pltpu.make_async_copy(src, dst.at[t], local.at[1 + i])
        for i, (src, dst) in enumerate(((tok_in, tok), (dec_in, dec), (cot_in, cot)))
    ]
    for stay in stays:
        stay.start()
    own_wout = pltpu.make_async_copy(
        wout_in, wout_all.at[jnp.clip(s - t * own_blocks, 0, own_blocks - 1)], local.at[4]
    )

    @pl.when(held(z))
    def _():
        own_wout.start()

    for k in range(n_tm):

        @pl.when(t == k)
        def _(k=k):
            lo, hi = k * width, (k + 1) * width
            par[0:taps, 0:width] = conv_in[:, lo:hi]
            par[taps : taps + 1, 0:width] = gain_in[:, lo:hi]

    par[0:taps, width:] = conv_in[:, inner:]
    own_win.wait()
    for k in range(n_tm):

        @pl.when(t == k)
        def _(k=k):
            lo, hi = k * width, (k + 1) * width
            win_all[s, :, 0:width] = win_own[:, lo:hi]
            win_all[s, :, width : 2 * width] = win_own[:, inner + lo : inner + hi]

    win_all[s, :, 2 * width :] = win_own[:, 2 * inner :]
    greet(tm_peers + stream_peers)
    targets = (s + 2, s - 2, sibling)

    def in_copy(slot, way):
        return pltpu.make_async_remote_copy(
            src_ref=win_all.at[slot], dst_ref=win_all.at[slot],
            send_sem=in_send.at[way, slot], recv_sem=in_recv.at[slot],
            device_id={"stream": targets[way]}, device_id_type=MESH,
        )

    def out_copy(slot, way):
        at = slot - t * own_blocks
        return pltpu.make_async_remote_copy(
            src_ref=wout_all.at[at], dst_ref=wout_all.at[at],
            send_sem=out_send.at[way, at], recv_sem=out_recv.at[at],
            device_id={"stream": targets[way]}, device_id_type=MESH,
        )

    def tm_copy(kind, peer, slot):
        src, dst = ((tok_in, tok), (dec_in, dec), (cot_in, cot))[kind]
        return pltpu.make_async_remote_copy(
            src_ref=src, dst_ref=dst.at[slot],
            send_sem=tm_send.at[kind, peer], recv_sem=tm_recv.at[kind, slot],
            device_id={"tm": peer}, device_id_type=MESH,
        )

    def passes(copy, pair, fits, act):
        slot = 2 * pair + c

        @pl.when(fits & (pair <= z) & (z < pairs - 1))
        def _():
            act(copy(slot, 0))

        @pl.when(fits & (pair >= z) & (z > 0))
        def _():
            act(copy(slot, 1))

        @pl.when(fits)
        def _():
            act(copy(slot, 2))

    def start(copy):
        copy.start()

    def relay(copy, j, fits):
        for pair, inside in ((z - j, z - j >= 0), (z + j, z + j < pairs)):
            inside = inside & fits(pair)

            @pl.when(inside)
            def _(pair=pair):
                copy(2 * pair + c, 2).wait_recv()

            passes(copy, pair, inside, start)

    passes(in_copy, z, z >= 0, start)
    for kind in (1, 0):
        for _, peer in tm_peers:
            tm_copy(kind, peer, t).start()

    @pl.when(held(z))
    def _():
        own_wout.wait()

    passes(out_copy, z, held(z), start)
    for _, peer in tm_peers:
        tm_copy(2, peer, t).start()
    for stay in stays:
        stay.wait()
    share = model // n_stream
    part = share // n_tm
    to = lax.broadcasted_iota(jnp.int32, (model, model), 0)
    source = lax.broadcasted_iota(jnp.int32, (model, model), 1)
    owner = to // share
    within = to - owner * share
    slab = within // part
    wanted = slab * (part * n_stream) + owner * part + (within - slab * part)
    permute[...] = jnp.where(source == wanted, 1.0, 0.0).astype(BF16)
    conv_w = [par[k : k + 1, :] for k in range(taps)]
    gain = par[taps : taps + 1, :width]
    row_i = lax.broadcasted_iota(jnp.int32, (rows, rows), 0)
    col_i = lax.broadcasted_iota(jnp.int32, (rows, rows), 1)
    causal = row_i >= col_i
    tril = jnp.where(causal, 1.0, 0.0).astype(F32)
    pick_row = lax.broadcasted_iota(jnp.int32, (all_heads, width), 0) - t * heads
    pick_col = lax.broadcasted_iota(jnp.int32, (all_heads, width), 1)
    spread = jnp.where(
        (pick_col >= pick_row * head_dim) & (pick_col < (pick_row + 1) * head_dim), 1.0, 0.0
    ).astype(F32)
    few = (heads + 7) // 8 * 8
    one_row = lax.broadcasted_iota(jnp.int32, (few, all_heads), 0)
    one_col = lax.broadcasted_iota(jnp.int32, (few, all_heads), 1) - t * heads
    single = jnp.where((one_row == one_col) & (one_row < heads), 1.0, 0.0).astype(F32)
    triu = jnp.where(row_i <= col_i, 1.0, 0.0).astype(F32)
    skip = mm_exact(jnp.broadcast_to(skip_in[...], (8, all_heads)), spread)[0:1, :]
    wide = width + 2 * states

    def prepare(q):
        here = slice(q * rows, (q + 1) * rows)
        log_decay = jnp.log(dec[q])
        total = mm_exact(tril, mm_exact(log_decay, spread, 0))
        across = mm_exact(mm_exact(single, log_decay), triu)
        last = total[rows - 1 : rows, :]
        g_s[here, :] = jnp.exp(total)
        f_s[here, :] = jnp.exp(last - total)
        el_s[q] = jnp.broadcast_to(jnp.exp(last), (8, width))
        for h in range(heads):
            lo = h * head_dim
            gap = total[:, lo : lo + 1] - across[h : h + 1, :]
            weight = jnp.where(causal, jnp.exp(jnp.where(causal, gap, 0.0)), 0.0)
            decay_s[q * heads + h] = weight.astype(BF16)

    for _, peer in tm_peers:
        tm_copy(1, peer, peer).wait_recv()
    for j in range(1, pairs):
        if j <= blocks:
            prepare(j - 1)
        relay(in_copy, j, lambda pair: pair >= 0)
    for q in range(pairs - 1, blocks):
        prepare(q)

    def copy(src, dst, send, recv, axis, peer, at, slot):
        return pltpu.make_async_remote_copy(
            src_ref=src.at[at], dst_ref=dst.at[slot],
            send_sem=send.at[peer], recv_sem=recv.at[slot],
            device_id={axis: peer}, device_id_type=MESH,
        )

    def s_copy(peer, slot):
        return copy(sums_s, sums_s, s_send, s_recv, "tm", peer, t, slot)

    def o_copy(peer, slot):
        return copy(osend, orecv, o_send, o_recv, "tm", peer, peer, slot)

    def g_copy(peer, slot):
        return copy(gsend, grecv, g_send, g_recv, "tm", peer, peer, slot)

    def p_copy(peer, slot):
        return copy(psend, precv, p_send, p_recv, "stream", peer, peer, slot)

    def a_copy(peer, slot):
        return copy(asend, arecv, a_send, a_recv, "tm", peer, peer, slot)

    state_s[...] = jnp.zeros_like(state_s)

    for pair in range(pairs):
        in_copy(2 * pair + 1 - c, 2).wait_recv()
    height = win_all.shape[1]
    for i in range(n_stream):
        win[i * height : (i + 1) * height, :] = win_all[i]
    for _, peer in tm_peers:
        tm_copy(0, peer, peer).wait_recv()

    def forward(q, carry):
        at = pl.multiple_of(q * rows, rows)
        here = pl.ds(at, rows)
        projected = mm(tok[q], win[...]).astype(BF16).astype(F32)
        gate = projected[:, :width]
        gate_s[here, :] = gate
        mixed = projected[:, width:]
        ext = jnp.concatenate([carry, mixed], axis=0)
        pre = conv_w[0] * ext[9 - taps : 9 - taps + rows]
        for k in range(1, taps):
            pre = pre + conv_w[k] * ext[9 - taps + k : 9 - taps + k + rows]
        pre_s[here, :] = pre
        conv = (pre * sigmoid(pre)).astype(BF16)
        x, b, c = conv[:, :width], conv[:, width : width + states], conv[:, width + states :]
        x_s[here, :] = x
        b_s[here, :] = b
        c_s[here, :] = c
        grow, fade, end = g_s[here, :], f_s[here, :], el_s[q][0:1, :]
        x32 = x.astype(F32)
        faded = (fade * x32).astype(BF16)
        fx_s[here, :] = faded
        before = state_s[...]
        held_low = before.astype(BF16)
        start_s[q] = held_low
        state_s[...] = end * before + mm_tn(b, faded)
        scores = mm_nt(c, b)
        inside = []
        for h in range(heads):
            lo = h * head_dim
            weight = decay_s[q * heads + h].astype(F32)
            mix = (weight * scores).astype(BF16)
            mask_s[q * heads + h] = mix
            inside.append(mm(mix, x[:, lo : lo + head_dim]))
        ssm = jnp.concatenate(inside, axis=1) + grow * mm(c, held_low) + skip * x32
        ssm_s[here, :] = ssm

        @pl.when(q + 1 < pairs)
        def _():
            relay(out_copy, q + 1, held)

        return mixed[rows - 8 :]

    lax.fori_loop(0, blocks, forward, jnp.zeros((8, wide), F32))
    for j in range(blocks + 1, pairs):
        relay(out_copy, j, held)
    for j in range(own_pairs):
        out_copy(2 * (t * own_pairs + j) + 1 - c, 2).wait_recv()
    height = wout_all.shape[1]
    for i in range(own_blocks):
        wout[i * height : (i + 1) * height, :] = wout_all[i]
    for _, peer in tm_peers:
        tm_copy(2, peer, peer).wait_recv()

    def inward(q, carry):
        here = pl.ds(pl.multiple_of(q * rows, rows), rows)
        gate = gate_s[here, :]
        gated = ssm_s[here, :] * (gate * sigmoid(gate))
        weighted = mm_nt(cot[q], wout[...]) * gain
        gw_s[here, :] = weighted
        square = jnp.sum(gated * gated, axis=1, keepdims=True)
        cross = jnp.sum(weighted * gated, axis=1, keepdims=True)
        pair = jnp.where(col_i == 0, square, jnp.where(col_i == 1, cross, 0.0))
        sums_s[t, q] = pair.T[0:8, :]
        return carry

    lax.fori_loop(0, blocks, inward, 0)

    for _, peer in tm_peers:
        s_copy(peer, t).start()
    for _, peer in tm_peers:
        s_copy(peer, peer).wait_recv()

    def normed_rows(q):
        both = sums_s[0, q]
        for k in range(1, n_tm):
            both = both + sums_s[k, q]
        columns = jnp.concatenate([both, jnp.zeros((rows - 8, rows), F32)], axis=0).T
        factor = lax.rsqrt(columns[:, 0:1] * (1.0 / inner) + 1e-05)
        return factor, columns[:, 1:2]

    def outward(q, carry):
        here = pl.ds(pl.multiple_of(q * rows, rows), rows)
        factor, _ = normed_rows(q)
        gate = gate_s[here, :]
        normed = (ssm_s[here, :] * (gate * sigmoid(gate)) * factor * gain).astype(BF16)
        nb_s[here, :] = normed
        return carry

    lax.fori_loop(0, blocks, outward, 0)

    def result(step, carry):
        q = lax.rem(t + 1 + step, blocks)
        here = pl.ds(pl.multiple_of(q * rows, rows), rows)
        osend[q] = mm(nb_s[here, :], wout[...]).astype(BF16)

        @pl.when(q != t)
        def _():
            o_copy(q, t).start()

        return carry

    lax.fori_loop(0, blocks, result, 0)

    product = mm_tn(cot[0], nb_s[0:rows, :])
    for q in range(1, blocks):
        product = product + mm_tn(cot[q], nb_s[q * rows : (q + 1) * rows, :])
    product = product.astype(BF16)
    psend[...] = mm(permute[...], product).astype(BF16).reshape(n_stream, share, width)
    for _, peer in stream_peers:
        p_copy(peer, s).start()

    state_s[...] = jnp.zeros_like(state_s)

    def backward(step, carry):
        q = blocks - 1 - step
        at = pl.multiple_of(q * rows, rows)
        here = pl.ds(at, rows)
        factor, cross = normed_rows(q)
        gate = gate_s[here, :]
        ssm = ssm_s[here, :]
        sig = sigmoid(gate)
        silu = gate * sig
        gated = ssm * silu
        grad_gated = gw_s[here, :] * factor - gated * (
            factor * factor * factor * cross * (1.0 / inner)
        )
        grad_ssm = grad_gated * silu
        grad_gate = grad_gated * ssm * (sig * (1.0 + gate * (1.0 - sig)))
        x, b, c = x_s[here, :], b_s[here, :], c_s[here, :]
        low = grad_ssm.astype(BF16)
        grown = (g_s[here, :] * grad_ssm).astype(BF16)
        adjoint = state_s[...]
        adjoint_low = adjoint.astype(BF16)
        state_s[...] = el_s[q][0:1, :] * adjoint + mm_tn(c, grown)
        through = []
        gap = jnp.zeros((rows, rows), F32)
        for h in range(heads):
            lo = h * head_dim
            part_low = low[:, lo : lo + head_dim]
            through.append(mm_tn(mask_s[q * heads + h], part_low))
            gap = gap + mm_nt(part_low, x[:, lo : lo + head_dim]) * decay_s[
                q * heads + h
            ].astype(F32)
        gap = gap.astype(BF16)
        grad_x = (
            jnp.concatenate(through, axis=1)
            + f_s[here, :] * mm(b, adjoint_low)
            + skip * grad_ssm
        )
        grad_c = mm(gap, b) + mm_nt(grown, start_s[q])
        grad_b = mm_tn(gap, c) + mm_nt(fx_s[here, :], adjoint_low)
        pre = pre_s[here, :]
        sig_pre = sigmoid(pre)
        grad_pre = jnp.concatenate([grad_x, grad_b, grad_c], axis=1) * (
            sig_pre * (1.0 + pre * (1.0 - sig_pre))
        )
        ext = jnp.concatenate([grad_pre, carry], axis=0)
        grad_mix = conv_w[taps - 1] * ext[0:rows]
        for k in range(taps - 1):
            grad_mix = grad_mix + conv_w[k] * ext[taps - 1 - k : taps - 1 - k + rows]
        grad_proj = jnp.concatenate([grad_gate.astype(BF16), grad_mix.astype(BF16)], axis=1)
        gsend[q] = mm_nt(grad_proj, win[...]).astype(BF16)

        @pl.when(q != t)
        def _():
            g_copy(q, t).start()

        return grad_pre[0:8]

    lax.fori_loop(0, blocks, backward, jnp.zeros((8, width + 2 * states), F32))

    for _, peer in stream_peers:
        p_copy(peer, peer).wait_recv()
    total = psend[s].astype(F32)
    for _, peer in stream_peers:
        total = total + precv[peer].astype(F32)
    for k in range(n_tm):
        asend[k] = total[k * part : (k + 1) * part, :]
    for _, peer in tm_peers:
        a_copy(peer, t).start()
    for _, peer in tm_peers:
        o_copy(peer, peer).wait_recv()
    total = osend[t].astype(F32)
    for _, peer in tm_peers:
        total = total + orecv[peer].astype(F32)
    out[...] = total.astype(BF16)
    for _, peer in tm_peers:
        g_copy(peer, peer).wait_recv()
    total = gsend[t].astype(F32)
    for _, peer in tm_peers:
        total = total + grecv[peer].astype(F32)
    grad_tok[...] = total.astype(BF16)
    for _, peer in tm_peers:
        a_copy(peer, peer).wait_recv()
    arecv[t] = asend[t]
    scale = (n_stream * blocks * rows) ** (-0.5)
    grad_out_t[...] = (
        jnp.concatenate([arecv[k] for k in range(n_tm)], axis=1) * scale
    )
    for _, peer in tm_peers:
        s_copy(peer, t).wait_send()
        o_copy(peer, t).wait_send()
        g_copy(peer, t).wait_send()
        a_copy(peer, t).wait_send()
    for _, peer in stream_peers:
        p_copy(peer, s).wait_send()
    for pair in range(pairs):
        passes(in_copy, pair, z >= 0, lambda copy: copy.wait_send())
    for pair in range(pairs):
        passes(out_copy, pair, held(pair), lambda copy: copy.wait_send())
    for kind in range(3):
        for _, peer in tm_peers:
            tm_copy(kind, peer, t).wait_send()


def shards(n_tm, n_stream, tokens, cotangent, decay, in_w, out_w, conv_w, dskip, norm_w):
    rows, model = tokens.shape[1:]
    all_heads = dskip.shape[0]
    inner = norm_w.shape[0]
    states = (in_w.shape[1] - 2 * inner) // 2
    taps = conv_w.shape[0]
    heads = all_heads // n_tm
    head_dim = inner // all_heads
    width = heads * head_dim
    wide = width + 2 * states
    span = width + wide
    own_blocks = width // out_w.shape[0]
    vmem = pl.BlockSpec(memory_space=pltpu.VMEM)
    hbm = pl.BlockSpec(memory_space=pltpu.HBM)
    dma = pltpu.SemaphoreType.DMA
    length = n_tm * rows
    share = model // n_stream
    part = share // n_tm
    V = pltpu.VMEM
    out, grad_tok, grad_out_t = pl.pallas_call(
        functools.partial(
            layer_kernel, n_tm, n_stream, inner, heads, head_dim, states, taps
        ),
        out_shape=[
            jax.ShapeDtypeStruct((rows, model), BF16),
            jax.ShapeDtypeStruct((rows, model), BF16),
            jax.ShapeDtypeStruct((part, inner), F32),
        ],
        in_specs=[hbm] * 5 + [vmem] * 3,
        out_specs=[vmem] * 3,
        scratch_shapes=[
            V((n_tm, rows, model), BF16), V((n_tm, rows, model), BF16),
            V((n_tm, all_heads, rows), F32), V(in_w.shape, BF16),
            V((n_stream, in_w.shape[0], span), BF16), V((own_blocks, out_w.shape[0], model), BF16),
            V((model, span), BF16), V((width, model), BF16), V((8, wide), F32),
            V((model, model), BF16),
            V((length, width), F32), V((length, wide), F32),
            V((length, width), BF16), V((length, states), BF16),
            V((length, states), BF16), V((length, width), F32), V((length, width), F32),
            V((n_tm, 8, width), F32), V((length, width), F32), V((length, width), F32),
            V((length, width), BF16), V((n_tm * heads, rows, rows), BF16),
            V((n_tm * heads, rows, rows), BF16), V((n_tm, states, width), BF16),
            V((length, width), BF16), V((states, width), F32),
            V((n_tm, n_tm, 8, rows), F32),
            V((n_tm, rows, model), BF16), V((n_tm, rows, model), BF16),
            V((n_tm, rows, model), BF16), V((n_tm, rows, model), BF16),
            V((n_stream, share, width), BF16), V((n_stream, share, width), BF16),
            V((n_tm, part, width), F32), V((n_tm, part, width), F32),
            dma((5,)), dma((3, n_tm)), dma((3, n_tm)), dma((3, n_stream)), dma((n_stream,)),
            dma((3, own_blocks)), dma((own_blocks,)),
            dma((n_tm,)), dma((n_tm,)), dma((n_tm,)), dma((n_tm,)), dma((n_tm,)), dma((n_tm,)),
            dma((n_stream,)), dma((n_stream,)), dma((n_tm,)), dma((n_tm,)),
        ],
        compiler_params=pltpu.CompilerParams(
            collective_id=0, has_side_effects=True, vmem_limit_bytes=60 * 2**20
        ),
        name="layer",
    )(
        tokens[0], cotangent[0], decay[0].T, in_w, out_w, conv_w, norm_w[None], dskip[None]
    )
    return out[None], grad_tok[None], grad_out_t


def solution(mesh):
    in_specs = (
        P("stream", "tm", None),
        P("stream", "tm", None),
        P("stream", "tm", None),
        P("stream", None),
        P("stream", None),
        P(),
        P(),
        P(),
    )
    out_specs = (P("stream", "tm", None), P("stream", "tm", None), P(("tm", "stream"), None))
    return jax.shard_map(
        functools.partial(shards, mesh.shape["tm"], mesh.shape["stream"]),
        mesh=mesh, in_specs=in_specs, out_specs=out_specs, check_vma=False,
    )
```

time: 77.8 us -> 72.5 us (0.932)
  local copies, waits for them, and re-layouts: 10.4 us -> 4.6 us
  Pallas kernels: 66.2 us -> 67 us
    pallas_call x1, Pallas kernels: 38.2 us -> 67 us  [shards(): pl.pallas_call(functools.partial(layer_kernel, n_tm, n_stream, inner, hea...]
    pallas_call x1 -> x0, Pallas kernels: 27.9 us -> none  [shards(): pl.pallas_call(functools.partial(gather_kernel, n_tm, n_stream, own_block...]
    dynamic_slice x4 -> x0, local copies, waits for them, and re-layouts: 3.14 us -> none  [the longest x3 2.41 us: mine(): return lax.dynamic_slice_in_dim(a, offset + t * width, width, axis)]
    unnamed x10 -> x7, local copies, waits for them, and re-layouts: 5.63 us -> 3.3 us
    slice x2 -> x0, local copies, waits for them, and re-layouts: 1.49 us -> none  [the longest x1 0.81 us: shards(): in_w[:, 2 * inner:]]
    broadcast_in_dim x3 -> x1, local copies, waits for them, and re-layouts: 0.08 us -> 1.3 us  [shards(): norm_w[None]]
where the time goes in v2:
time: 72.5 us; the launch traced here: 72.2 us
  Pallas kernels  67 us (92%)
  local copies, waits for them, and re-layouts  4.6 us (6%)
    pallas_call x1, Pallas kernels, shards(): pl.pallas_call(functools.partial(layer_kernel, n_tm, n_stream, inner, hea...  67 us
    unnamed x7, local copies, waits for them, and re-layouts  3.3 us

profile of v2, /device:TPU:0, one launch (start us, length us, event | category | flops | bytes accessed | tf_op | source)
XLA Modules:
  0.0 72.2 jit_solution(17718016900857125750)
XLA Ops:
  0.6 1.3 %broadcast_in_dim.12.gain_in = f32[1,1536]{1,0:T(1,128)} reshape(f32[1536]{0:T(1024)} %param.15) | data formatting | bytes 12288 | tf_op jit(solution)/shard_map/broadcast_in_dim | solution.py:534
  1.9 67.0 %layer.1 = (bf16[128,768]{1,0:T(8,128)(2,1)}, bf16[128,768]{1,0:T(8,128)(2,1)}, f32[24,1536]{1,0:T(8,128)}) custom-call(bf16[128,768]{1,0:T(8,128)(2,1)} %bitcast.8, bf16[128,768]{1,0:T(8,128)(2,1)} %bitcast.9, f32[24,128]{1,0:T(8,128)} %bitcast.12, bf16[96,3328]{1,0:T(8,128)(2,1)} %win_in.1, bf16[192,768]{1,0:T(8,128)(2,1)} %wout_in.1, f32[4,1792]{1,0:T(4,128)} %conv_in.1, ...), custom_call_target="tpu_custom_call" | custom-call | tf_op jit(solution)/shard_map/layer/pallas_call | solution.py:495
  68.9 0.0 copy-start
  68.9 1.7 %copy.14 = bf16[1,128,768]{2,1,0:T(8,128)(2,1)} copy(bf16[1,128,768]{2,1,0:T(8,128)(2,1)} %bitcast.11) | data formatting | bytes 393216
  70.6 0.0 copy-done
  70.6 0.0 copy-start.1
  70.6 0.7 copy.15
  71.3 0.3 copy-done.1
  71.6 0.7 copy.16
Async XLA Ops:
  68.9 1.7 %copy-start = (bf16[128,768]{1,0:T(8,128)(2,1)S(1)}, bf16[128,768]{1,0:T(8,128)(2,1)}, u32[]{:S(2)}) copy-start(bf16[128,768]{1,0:T(8,128)(2,1)} %get-tuple-element.7) | copy-start | bytes 589828
  70.6 1.0 %copy-start.1 = (f32[24,1536]{1,0:T(8,128)S(1)}, f32[24,1536]{1,0:T(8,128)}, u32[]{:S(2)}) copy-start(f32[24,1536]{1,0:T(8,128)} %get-tuple-element.14) | copy-start | bytes 442372
